TPU v7x, 32 devices: a whole 2x2x4 slice. The times are simulated.
32 devices in a mesh: seq: 16 (over z, y, x), head: 2 (over core).
Axes of the slice: x: 2, y: 2, z: 4, core: 2. Of those that a mesh axis runs over, the one named last changes fastest.
Arguments:
- q_delta: bfloat16 [4096, 2048], P('seq', 'head'), may hold values from -6 to 6
- k_delta: bfloat16 [4096, 2048], P('seq', 'head'), may hold values from -6 to 6
- v_delta: bfloat16 [4096, 2048], P('seq', 'head'), may hold values from -6 to 6
- write_rate: float32 [4096, 16], P('seq', 'head'), may hold values from 0 to 1
- q_attn: bfloat16 [4096, 2048], P('seq', 'head'), may hold values from -200 to 200
- k_attn: bfloat16 [4096, 2048], P('seq', 'head'), may hold values from -6 to 6
- out_gain: float32 [2048], P('head'), may hold values from 0.5 to 1.5
Outputs:
- delta_out: bfloat16 [4096, 2048], P('seq', 'head')
- normed_out: bfloat16 [4096, 2048], P('seq', 'head')
All inputs are finite; a program needn't handle non-finite values.
Results may differ from a plain program's by a relative error of at most 0.0058.
Values may be sent and summed in bfloat16 or wider, within the bound.
A program may use at most 64 MiB of HBM per device.

v0:
```python
import math

import jax
import jax.numpy as jnp
from jax import lax
from jax.sharding import PartitionSpec as P

GROUP_TOKENS = 64
WINDOW = 2048


highest = lax.Precision.HIGHEST


def shifted(value, axis, by):
    size = lax.axis_size(axis)
    pairs = [(i, i + by) for i in range(size) if 0 <= i + by < size]
    return lax.ppermute(value, axis, pairs)


def unit_rows(entries):
    entries = entries.astype(jnp.float32)
    return entries * lax.rsqrt(jnp.sum(entries * entries, axis=-1, keepdims=True) + 1e-06)


def lower_inverse(below_part):
    length = below_part.shape[-1]
    identity = jnp.eye(length, dtype=jnp.float32)
    result = identity - below_part
    raised = below_part
    doubled = 2
    while doubled < length:
        raised = jnp.einsum("nij,njk->nik", raised, raised, precision=highest)
        result = jnp.einsum("nij,njk->nik", result, identity + raised, precision=highest)
        doubled = doubled * 2
    return result


def prepare(queries, key_rows, values, rate_rows):
    n_groups = queries.shape[0] // GROUP_TOKENS
    q_unit = unit_rows(queries).reshape(n_groups, GROUP_TOKENS, -1)
    k_unit = unit_rows(key_rows).reshape(n_groups, GROUP_TOKENS, -1)
    val_units = values.astype(jnp.float32).reshape(n_groups, GROUP_TOKENS, -1)
    rate_col = rate_rows.reshape(n_groups, GROUP_TOKENS, 1)
    key_inner = jnp.einsum("nik,njk->nij", k_unit, k_unit, precision=highest)
    positions = jnp.arange(GROUP_TOKENS)
    is_below = positions[:, None] > positions[None, :]
    on_or_below = positions[:, None] >= positions[None, :]
    below_part = jnp.where(is_below[None], rate_col * key_inner, 0.0)
    inverse = lower_inverse(below_part)
    writes = jnp.einsum("nij,njk->nik", inverse, rate_col * k_unit, precision=highest)
    updates = jnp.einsum("nij,njk->nik", inverse, rate_col * val_units, precision=highest)
    query_key = jnp.where(
        on_or_below[None], jnp.einsum("nik,njk->nij", q_unit, k_unit, precision=highest), 0.0
    )
    return (q_unit, k_unit, writes, updates, query_key)


def local_pair(k_unit, writes, updates):
    head_size = k_unit.shape[-1]
    identity = jnp.eye(head_size, dtype=jnp.float32)

    def stride(carry, inputs_now):
        transit, carried = carry
        k_block, w_block, u_block = inputs_now
        stepped = identity - jnp.dot(k_block.T, w_block, precision=highest)
        transit = jnp.dot(stepped, transit, precision=highest)
        carried = jnp.dot(stepped, carried, precision=highest) + jnp.dot(
            k_block.T, u_block, precision=highest
        )
        return ((transit, carried), None)

    start_pair = (identity, jnp.zeros((head_size, head_size), jnp.float32))
    (transit, carried), _ = lax.scan(stride, start_pair, (k_unit, writes, updates))
    return (transit, carried)


def advance(carried, inputs_now):
    q_block, k_block, w_block, u_block, cross_block = inputs_now
    corrected = u_block - jnp.dot(w_block, carried, precision=highest)
    result_now = jnp.dot(q_block, carried, precision=highest) + jnp.dot(
        cross_block, corrected, precision=highest
    )
    return (carried + jnp.dot(k_block.T, corrected, precision=highest), result_now)


def run_blocks(carried_in, q_unit, k_unit, writes, updates, query_key):
    _, results = lax.scan(advance, carried_in, (q_unit, k_unit, writes, updates, query_key))
    return results


def batched_dot(left, right):
    return jnp.einsum("hij,hjk->hik", left, right, precision=highest)


def on_device(q_delta, k_delta, v_delta, write_rate, q_attn, k_attn, out_gain):
    tok_rows, features = q_delta.shape
    heads_here = write_rate.shape[1]
    head_size = features // heads_here

    def by_head(entries):
        return entries.reshape(tok_rows, heads_here, head_size).transpose(1, 0, 2)

    q_unit, k_unit, writes, updates, query_key = jax.vmap(prepare)(
        by_head(q_delta), by_head(k_delta), by_head(v_delta), write_rate.T
    )
    transit, carried = jax.vmap(local_pair)(k_unit, writes, updates)
    position = lax.axis_index("seq")

    def relay(loop_index, received):
        leaving = batched_dot(transit, received) + carried
        arrived = shifted(leaving, "seq", 1)
        return jnp.where(position == loop_index + 1, arrived, received)

    incoming = lax.fori_loop(0, lax.axis_size("seq") - 1, relay, jnp.zeros_like(carried))
    results = jax.vmap(run_blocks)(incoming, q_unit, k_unit, writes, updates, query_key)
    delta_out = (
        results.reshape(heads_here, tok_rows, head_size)
        .transpose(1, 0, 2)
        .reshape(tok_rows, features)
        .astype(jnp.bfloat16)
    )
    own_rows = jnp.stack((k_attn, delta_out))
    shard_reach = WINDOW // tok_rows
    pieces = [own_rows]
    for hop_count in range(1, shard_reach + 1):
        pieces = [shifted(own_rows, "seq", hop_count)] + pieces
    rows_all = jnp.concatenate(pieces, axis=1)
    block_rows = min(512, tok_rows)
    first_row = lax.axis_index("seq") * tok_rows
    score_scale = 1.0 / math.sqrt(head_size)

    def attend_block(block_start):
        queries = q_attn.reshape(block_rows, heads_here, head_size)
        near_keys = rows_all[0].reshape(WINDOW + block_rows, heads_here, head_size)
        near_values = rows_all[1].reshape(WINDOW + block_rows, heads_here, head_size)
        scores = (
            jnp.einsum("qhd,khd->hqk", queries, near_keys, preferred_element_type=jnp.float32)
            * score_scale
        )
        q_index = jnp.arange(block_rows)[:, None]
        k_index = jnp.arange(WINDOW + block_rows)[None, :]
        allowed = (
            (k_index > q_index)
            & (k_index <= q_index + WINDOW)
            & (first_row + block_start + k_index >= WINDOW)
        )
        row_top = jnp.max(jnp.where(allowed[None], scores, -1e30), axis=2, keepdims=True)
        exps = jnp.exp(jnp.where(allowed[None], scores - row_top, -1e30))
        weights = (exps / jnp.sum(exps, axis=2, keepdims=True)).astype(jnp.bfloat16)
        mixed_rows = jnp.einsum(
            "hqk,khd->qhd", weights, near_values, preferred_element_type=jnp.float32
        )
        return mixed_rows.reshape(block_rows, features)

    starts = jnp.arange(tok_rows // block_rows) * block_rows
    attended = lax.map(attend_block, starts).reshape(tok_rows, features)
    squares = jnp.sum(attended * attended, axis=1)
    total_sq = lax.psum(squares, "head")
    scale_rows = lax.rsqrt(total_sq / (features * lax.axis_size("head")) + 1e-06)
    normed_out = (attended * out_gain[None, :] * scale_rows[:, None]).astype(jnp.bfloat16)
    return (delta_out, normed_out)


def solution(mesh):
    placed = (
        P("seq", "head"),
        P("seq", "head"),
        P("seq", "head"),
        P("seq", "head"),
        P("seq", "head"),
        P("seq", "head"),
        P("head"),
    )
    return jax.shard_map(
        on_device,
        mesh=mesh,
        in_specs=placed,
        out_specs=(P("seq", "head"), P("seq", "head")),
        check_vma=False,
    )
```

profile of v0, /device:TPU:25, one launch (start us, length us, event | category | flops | bytes accessed | tf_op | source)
XLA Modules:
  0.0 674.7 jit_solution(7545037934482250465)
XLA Ops:
  10.8 2.5 copy.42
  13.4 2.0 copy.55
  35.2 22.3 %while.44 = (s32[]{:T(128)}, f32[8,128,128]{2,1,0:T(8,128)S(1)}, f32[8,128,128]{2,1,0:T(8,128)S(1)}, f32[4,8,64,128]{3,2,1,0:T(8,128)}, f32[4,8,64,128]{3,2,1,0:...) while((s32[]{:T(128)}, f32[8,128,128]{2,1,0:T(8,128)S(1)}, ...), condition=%wide.region_2.3_spmd.clone, body=%wide.region_1.0_spmd.clone.sunk | while | flops 604405760 | bytes 7997543 | solution.py:74
  35.5 2.0 convolution_subtract_fusion.5
  37.6 2.0 fusion.180
  41.0 2.0 convolution_subtract_fusion.5
  43.1 2.0 fusion.180
  46.6 2.0 convolution_subtract_fusion.5
  48.6 2.0 fusion.180
  52.1 2.0 convolution_subtract_fusion.5
  54.1 2.0 fusion.180
  57.5 3.9 fusion.51
  61.4 228.3 %while.45 = (s32[]{:T(128)}, f32[8,128,128]{2,1,0:T(8,128)S(1)}, s32[]{:T(128)}, f32[8,128,128]{2,1,0:T(8,128)S(1)}, f32[8,128,128]{2,1,0:T(8,128)S(1)}, /*index=5*/s32[]{:T(128)}, s32[]{:T(128)}) while((s32[]{:T(128)}, f32[8,128,128]{2,1,0:T(8,128)S(1)}, s32[]{:T(128)}, f32[8,128,128]{2,1,0:T(8,128)S(1)}, ...), condition=%wide.region_4.5_spmd.clone, body=%wide.region_3.4_spmd.clone.sunk | while | flops 201850880 | bytes 5767306 | solution.py:115
  62.1 3.1 collective-permute-start
  65.2 13.3 %collective-permute-done = f32[8,128,128]{2,1,0:T(8,128)S(1)} collective-permute-done((f32[8,128,128]{2,1,0:T(8,128)S(1)}, f32[8,128,128]{2,1,0:T(8,128)S(1)}, u32[]{:S(2)}, u32[]{:S(2)}) %collective-permute-start) | collective-permute-done | bytes 524320 | tf_op jit(solution)/shard_map/while/body/eval_jaxpr/ppermute | solution.py:18
  81.3 13.6 %collective-permute-done = f32[8,128,128]{2,1,0:T(8,128)S(1)} collective-permute-done((f32[8,128,128]{2,1,0:T(8,128)S(1)}, f32[8,128,128]{2,1,0:T(8,128)S(1)}, u32[]{:S(2)}, u32[]{:S(2)}) %collective-permute-start) | collective-permute-done | bytes 524320 | tf_op jit(solution)/shard_map/while/body/eval_jaxpr/ppermute | solution.py:18
  97.7 12.7 %collective-permute-done = f32[8,128,128]{2,1,0:T(8,128)S(1)} collective-permute-done((f32[8,128,128]{2,1,0:T(8,128)S(1)}, f32[8,128,128]{2,1,0:T(8,128)S(1)}, u32[]{:S(2)}, u32[]{:S(2)}) %collective-permute-start) | collective-permute-done | bytes 524320 | tf_op jit(solution)/shard_map/while/body/eval_jaxpr/ppermute | solution.py:18
  113.2 11.8 %collective-permute-done = f32[8,128,128]{2,1,0:T(8,128)S(1)} collective-permute-done((f32[8,128,128]{2,1,0:T(8,128)S(1)}, f32[8,128,128]{2,1,0:T(8,128)S(1)}, u32[]{:S(2)}, u32[]{:S(2)}) %collective-permute-start) | collective-permute-done | bytes 524320 | tf_op jit(solution)/shard_map/while/body/eval_jaxpr/ppermute | solution.py:18
  127.7 10.9 %collective-permute-done = f32[8,128,128]{2,1,0:T(8,128)S(1)} collective-permute-done((f32[8,128,128]{2,1,0:T(8,128)S(1)}, f32[8,128,128]{2,1,0:T(8,128)S(1)}, u32[]{:S(2)}, u32[]{:S(2)}) %collective-permute-start) | collective-permute-done | bytes 524320 | tf_op jit(solution)/shard_map/while/body/eval_jaxpr/ppermute | solution.py:18
  141.3 9.8 %collective-permute-done = f32[8,128,128]{2,1,0:T(8,128)S(1)} collective-permute-done((f32[8,128,128]{2,1,0:T(8,128)S(1)}, f32[8,128,128]{2,1,0:T(8,128)S(1)}, u32[]{:S(2)}, u32[]{:S(2)}) %collective-permute-start) | collective-permute-done | bytes 524320 | tf_op jit(solution)/shard_map/while/body/eval_jaxpr/ppermute | solution.py:18
  153.9 9.8 %collective-permute-done = f32[8,128,128]{2,1,0:T(8,128)S(1)} collective-permute-done((f32[8,128,128]{2,1,0:T(8,128)S(1)}, f32[8,128,128]{2,1,0:T(8,128)S(1)}, u32[]{:S(2)}, u32[]{:S(2)}) %collective-permute-start) | collective-permute-done | bytes 524320 | tf_op jit(solution)/shard_map/while/body/eval_jaxpr/ppermute | solution.py:18
  166.4 9.8 %collective-permute-done = f32[8,128,128]{2,1,0:T(8,128)S(1)} collective-permute-done((f32[8,128,128]{2,1,0:T(8,128)S(1)}, f32[8,128,128]{2,1,0:T(8,128)S(1)}, u32[]{:S(2)}, u32[]{:S(2)}) %collective-permute-start) | collective-permute-done | bytes 524320 | tf_op jit(solution)/shard_map/while/body/eval_jaxpr/ppermute | solution.py:18
  179.0 10.8 %collective-permute-done = f32[8,128,128]{2,1,0:T(8,128)S(1)} collective-permute-done((f32[8,128,128]{2,1,0:T(8,128)S(1)}, f32[8,128,128]{2,1,0:T(8,128)S(1)}, u32[]{:S(2)}, u32[]{:S(2)}) %collective-permute-start) | collective-permute-done | bytes 524320 | tf_op jit(solution)/shard_map/while/body/eval_jaxpr/ppermute | solution.py:18
  192.6 11.9 %collective-permute-done = f32[8,128,128]{2,1,0:T(8,128)S(1)} collective-permute-done((f32[8,128,128]{2,1,0:T(8,128)S(1)}, f32[8,128,128]{2,1,0:T(8,128)S(1)}, u32[]{:S(2)}, u32[]{:S(2)}) %collective-permute-start) | collective-permute-done | bytes 524320 | tf_op jit(solution)/shard_map/while/body/eval_jaxpr/ppermute | solution.py:18
  207.3 13.0 %collective-permute-done = f32[8,128,128]{2,1,0:T(8,128)S(1)} collective-permute-done((f32[8,128,128]{2,1,0:T(8,128)S(1)}, f32[8,128,128]{2,1,0:T(8,128)S(1)}, u32[]{:S(2)}, u32[]{:S(2)}) %collective-permute-start) | collective-permute-done | bytes 524320 | tf_op jit(solution)/shard_map/while/body/eval_jaxpr/ppermute | solution.py:18
  223.1 14.1 %collective-permute-done = f32[8,128,128]{2,1,0:T(8,128)S(1)} collective-permute-done((f32[8,128,128]{2,1,0:T(8,128)S(1)}, f32[8,128,128]{2,1,0:T(8,128)S(1)}, u32[]{:S(2)}, u32[]{:S(2)}) %collective-permute-start) | collective-permute-done | bytes 524320 | tf_op jit(solution)/shard_map/while/body/eval_jaxpr/ppermute | solution.py:18
  239.9 15.3 %collective-permute-done = f32[8,128,128]{2,1,0:T(8,128)S(1)} collective-permute-done((f32[8,128,128]{2,1,0:T(8,128)S(1)}, f32[8,128,128]{2,1,0:T(8,128)S(1)}, u32[]{:S(2)}, u32[]{:S(2)}) %collective-permute-start) | collective-permute-done | bytes 524320 | tf_op jit(solution)/shard_map/while/body/eval_jaxpr/ppermute | solution.py:18
  257.9 14.9 %collective-permute-done = f32[8,128,128]{2,1,0:T(8,128)S(1)} collective-permute-done((f32[8,128,128]{2,1,0:T(8,128)S(1)}, f32[8,128,128]{2,1,0:T(8,128)S(1)}, u32[]{:S(2)}, u32[]{:S(2)}) %collective-permute-start) | collective-permute-done | bytes 524320 | tf_op jit(solution)/shard_map/while/body/eval_jaxpr/ppermute | solution.py:18
  275.6 13.9 %collective-permute-done = f32[8,128,128]{2,1,0:T(8,128)S(1)} collective-permute-done((f32[8,128,128]{2,1,0:T(8,128)S(1)}, f32[8,128,128]{2,1,0:T(8,128)S(1)}, u32[]{:S(2)}, u32[]{:S(2)}) %collective-permute-start) | collective-permute-done | bytes 524320 | tf_op jit(solution)/shard_map/while/body/eval_jaxpr/ppermute | solution.py:18
  289.7 28.9 %while.43 = (s32[]{:T(128)}, f32[8,128,128]{2,1,0:T(8,128)S(1)}, bf16[4,8,64,128]{3,2,0,1:T(8,128)(2,1)}, f32[4,8,64,128]{3,2,1,0:T(8,128)}, f32[4,8,64,128]{3,2...) while((s32[]{:T(128)}, f32[8,128,128]{2,1,0:T(8,128)S(1)}, ...), condition=%wide.region_7.8_spmd, body=%wide.region_6.7_spmd.sunk | while | flops 352583680 | bytes 4982893 | solution.py:88
  292.9 2.0 fusion.169
  300.1 2.0 fusion.169
  307.3 2.0 fusion.169
  314.5 2.0 fusion.169
  327.7 87.9 %collective-permute-done.3 = bf16[2,256,1024]{1,2,0:T(8,128)(2,1)} collective-permute-done((bf16[2,256,1024]{1,2,0:T(8,128)(2,1)S(1)}, bf16[2,256,1024]{1,2,0:T(8,128)(2,1)}, u32[]{:S(2)}, u32[]{:S(2)}) %collective-permute-start.3) | collective-permute-done | bytes 1048608 | tf_op jit(solution)/shard_map/ppermute | solution.py:18
  422.6 2.4 constant_dynamic-update-slice_fusion.8
  425.0 2.4 constant_dynamic-update-slice_fusion.7
  427.4 2.4 constant_dynamic-update-slice_fusion.6
  429.8 193.8 %collective-permute-done.4 = bf16[2,256,1024]{1,2,0:T(8,128)(2,1)} collective-permute-done((bf16[2,256,1024]{1,2,0:T(8,128)(2,1)S(1)}, bf16[2,256,1024]{1,2,0:T(8,128)(2,1)}, u32[]{:S(2)}, u32[]{:S(2)}) %collective-permute-start.4) | collective-permute-done | bytes 1048608 | tf_op jit(solution)/shard_map/ppermute | solution.py:18
  623.6 2.3 constant_dynamic-update-slice_fusion.5
  626.0 2.3 constant_dynamic-update-slice_fusion.4
  628.3 2.3 constant_dynamic-update-slice_fusion.3
  630.6 2.3 constant_dynamic-update-slice_fusion.2
  632.9 2.4 constant_dynamic-update-slice_fusion.1
  636.5 8.1 %fusion.91 = (bf16[1,2304,1024]{1,2,0:T(8,128)(2,1)}, bf16[1,2304,1024]{1,2,0:T(8,128)(2,1)}) fusion(bf16[2,2304,1024]{1,2,0:T(8,128)(2,1)} %constant_dynamic-update-slice_fusion), kind=kLoop, calls=%fused_computation.125 | loop fusion | bytes 18874368 | tf_op jit(solution)/shard_map/while/body/eval_jaxpr/slice | solution.py:135
  644.6 16.5 %fusion.92 = (f32[8,256]{1,0:T(8,128)S(1)}, f32[8,256,2304]{1,2,0:T(8,128)}) fusion(pred[256,2304]{0,1:T(8,128)(4,1)S(1)} %fusion.49, bf16[2304,8,128]{0,2,1:T(8,128)(2,1)} %bitcast.206, bf16[256,1024]{1,0:T(8,128)(2,1)S(1)} %copy-done), kind=kOutput, calls=%fused_computation.126 | convolution fusion | flops 2444232960 | bytes 24715264 | tf_op jit(solution)/shard_map/while/body/eval_jaxpr/sub | solution.py:149
  661.1 9.2 %fusion.52 = (f32[256]{0:T(256)S(1)}, f32[8,128,256]{2,1,0:T(8,128)S(1)}) fusion(bf16[2304,8,128]{0,2,1:T(8,128)(2,1)} %bitcast.205, f32[8,256,2304]{1,2,0:T(8,128)} %get-tuple-element.321, f32[8,256]{1,0:T(8,128)S(1)} %get-tuple-element.320), kind=kOutput, calls=%fused_computation.71 | convolution fusion | flops 1217920768 | bytes 24650752 | tf_op jit(solution)/shard_map/while/body/eval_jaxpr/hqk,khd->qhd/dot_general | solution.py:151
  670.4 2.6 psum.7
  (145 shorter events, 113.3 us)
Async XLA Ops:
  0.6 644.0 %copy-start = (bf16[256,1024]{1,0:T(8,128)(2,1)S(1)}, bf16[256,1024]{1,0:T(8,128)(2,1)}, u32[]{:S(2)}) copy-start(bf16[256,1024]{1,0:T(8,128)(2,1)} %param.17) | copy-start | bytes 1572868
  23.2 7.4 %copy-start.2 = (f32[8,256,128]{2,1,0:T(8,128)S(1)}, f32[8,256,128]{2,1,0:T(8,128)}, u32[]{:S(2)}) copy-start(f32[8,256,128]{2,1,0:T(8,128)} %copy.42) | copy-start | bytes 3145732
  62.1 16.5 %collective-permute-start = (f32[8,128,128]{2,1,0:T(8,128)S(1)}, f32[8,128,128]{2,1,0:T(8,128)S(1)}, u32[]{:S(2)}, u32[]{:S(2)}) collective-permute-start(f32[8,128,128]{2,1,0:T(8,128)S(1)} %convolution_add_fusion.10), channel_id=1, source_target_pairs={{0,2},{2,4},{4,6},{6,8},{8,10},{10,12},{12,14},{14,16},{16,18},{18... | collective-permute-start | bytes 1572872 | tf_op jit(solution)/shard_map/while/body/eval_jaxpr/ppermute | solution.py:18
  79.4 15.6 %collective-permute-start = (f32[8,128,128]{2,1,0:T(8,128)S(1)}, f32[8,128,128]{2,1,0:T(8,128)S(1)}, u32[]{:S(2)}, u32[]{:S(2)}) collective-permute-start(f32[8,128,128]{2,1,0:T(8,128)S(1)} %convolution_add_fusion.10), channel_id=1, source_target_pairs={{0,2},{2,4},{4,6},{6,8},{8,10},{10,12},{12,14},{14,16},{16,18},{18... | collective-permute-start | bytes 1572872 | tf_op jit(solution)/shard_map/while/body/eval_jaxpr/ppermute | solution.py:18
  95.8 14.6 %collective-permute-start = (f32[8,128,128]{2,1,0:T(8,128)S(1)}, f32[8,128,128]{2,1,0:T(8,128)S(1)}, u32[]{:S(2)}, u32[]{:S(2)}) collective-permute-start(f32[8,128,128]{2,1,0:T(8,128)S(1)} %convolution_add_fusion.10), channel_id=1, source_target_pairs={{0,2},{2,4},{4,6},{6,8},{8,10},{10,12},{12,14},{14,16},{16,18},{18... | collective-permute-start | bytes 1572872 | tf_op jit(solution)/shard_map/while/body/eval_jaxpr/ppermute | solution.py:18
  111.2 13.7 %collective-permute-start = (f32[8,128,128]{2,1,0:T(8,128)S(1)}, f32[8,128,128]{2,1,0:T(8,128)S(1)}, u32[]{:S(2)}, u32[]{:S(2)}) collective-permute-start(f32[8,128,128]{2,1,0:T(8,128)S(1)} %convolution_add_fusion.10), channel_id=1, source_target_pairs={{0,2},{2,4},{4,6},{6,8},{8,10},{10,12},{12,14},{14,16},{16,18},{18... | collective-permute-start | bytes 1572872 | tf_op jit(solution)/shard_map/while/body/eval_jaxpr/ppermute | solution.py:18
  125.8 12.8 %collective-permute-start = (f32[8,128,128]{2,1,0:T(8,128)S(1)}, f32[8,128,128]{2,1,0:T(8,128)S(1)}, u32[]{:S(2)}, u32[]{:S(2)}) collective-permute-start(f32[8,128,128]{2,1,0:T(8,128)S(1)} %convolution_add_fusion.10), channel_id=1, source_target_pairs={{0,2},{2,4},{4,6},{6,8},{8,10},{10,12},{12,14},{14,16},{16,18},{18... | collective-permute-start | bytes 1572872 | tf_op jit(solution)/shard_map/while/body/eval_jaxpr/ppermute | solution.py:18
  139.4 11.7 %collective-permute-start = (f32[8,128,128]{2,1,0:T(8,128)S(1)}, f32[8,128,128]{2,1,0:T(8,128)S(1)}, u32[]{:S(2)}, u32[]{:S(2)}) collective-permute-start(f32[8,128,128]{2,1,0:T(8,128)S(1)} %convolution_add_fusion.10), channel_id=1, source_target_pairs={{0,2},{2,4},{4,6},{6,8},{8,10},{10,12},{12,14},{14,16},{16,18},{18... | collective-permute-start | bytes 1572872 | tf_op jit(solution)/shard_map/while/body/eval_jaxpr/ppermute | solution.py:18
  152.0 11.7 %collective-permute-start = (f32[8,128,128]{2,1,0:T(8,128)S(1)}, f32[8,128,128]{2,1,0:T(8,128)S(1)}, u32[]{:S(2)}, u32[]{:S(2)}) collective-permute-start(f32[8,128,128]{2,1,0:T(8,128)S(1)} %convolution_add_fusion.10), channel_id=1, source_target_pairs={{0,2},{2,4},{4,6},{6,8},{8,10},{10,12},{12,14},{14,16},{16,18},{18... | collective-permute-start | bytes 1572872 | tf_op jit(solution)/shard_map/while/body/eval_jaxpr/ppermute | solution.py:18
  164.5 11.7 %collective-permute-start = (f32[8,128,128]{2,1,0:T(8,128)S(1)}, f32[8,128,128]{2,1,0:T(8,128)S(1)}, u32[]{:S(2)}, u32[]{:S(2)}) collective-permute-start(f32[8,128,128]{2,1,0:T(8,128)S(1)} %convolution_add_fusion.10), channel_id=1, source_target_pairs={{0,2},{2,4},{4,6},{6,8},{8,10},{10,12},{12,14},{14,16},{16,18},{18... | collective-permute-start | bytes 1572872 | tf_op jit(solution)/shard_map/while/body/eval_jaxpr/ppermute | solution.py:18
  177.1 12.8 %collective-permute-start = (f32[8,128,128]{2,1,0:T(8,128)S(1)}, f32[8,128,128]{2,1,0:T(8,128)S(1)}, u32[]{:S(2)}, u32[]{:S(2)}) collective-permute-start(f32[8,128,128]{2,1,0:T(8,128)S(1)} %convolution_add_fusion.10), channel_id=1, source_target_pairs={{0,2},{2,4},{4,6},{6,8},{8,10},{10,12},{12,14},{14,16},{16,18},{18... | collective-permute-start | bytes 1572872 | tf_op jit(solution)/shard_map/while/body/eval_jaxpr/ppermute | solution.py:18
  190.7 13.9 %collective-permute-start = (f32[8,128,128]{2,1,0:T(8,128)S(1)}, f32[8,128,128]{2,1,0:T(8,128)S(1)}, u32[]{:S(2)}, u32[]{:S(2)}) collective-permute-start(f32[8,128,128]{2,1,0:T(8,128)S(1)} %convolution_add_fusion.10), channel_id=1, source_target_pairs={{0,2},{2,4},{4,6},{6,8},{8,10},{10,12},{12,14},{14,16},{16,18},{18... | collective-permute-start | bytes 1572872 | tf_op jit(solution)/shard_map/while/body/eval_jaxpr/ppermute | solution.py:18
  205.4 14.9 %collective-permute-start = (f32[8,128,128]{2,1,0:T(8,128)S(1)}, f32[8,128,128]{2,1,0:T(8,128)S(1)}, u32[]{:S(2)}, u32[]{:S(2)}) collective-permute-start(f32[8,128,128]{2,1,0:T(8,128)S(1)} %convolution_add_fusion.10), channel_id=1, source_target_pairs={{0,2},{2,4},{4,6},{6,8},{8,10},{10,12},{12,14},{14,16},{16,18},{18... | collective-permute-start | bytes 1572872 | tf_op jit(solution)/shard_map/while/body/eval_jaxpr/ppermute | solution.py:18
  221.1 16.0 %collective-permute-start = (f32[8,128,128]{2,1,0:T(8,128)S(1)}, f32[8,128,128]{2,1,0:T(8,128)S(1)}, u32[]{:S(2)}, u32[]{:S(2)}) collective-permute-start(f32[8,128,128]{2,1,0:T(8,128)S(1)} %convolution_add_fusion.10), channel_id=1, source_target_pairs={{0,2},{2,4},{4,6},{6,8},{8,10},{10,12},{12,14},{14,16},{16,18},{18... | collective-permute-start | bytes 1572872 | tf_op jit(solution)/shard_map/while/body/eval_jaxpr/ppermute | solution.py:18
  238.0 17.2 %collective-permute-start = (f32[8,128,128]{2,1,0:T(8,128)S(1)}, f32[8,128,128]{2,1,0:T(8,128)S(1)}, u32[]{:S(2)}, u32[]{:S(2)}) collective-permute-start(f32[8,128,128]{2,1,0:T(8,128)S(1)} %convolution_add_fusion.10), channel_id=1, source_target_pairs={{0,2},{2,4},{4,6},{6,8},{8,10},{10,12},{12,14},{14,16},{16,18},{18... | collective-permute-start | bytes 1572872 | tf_op jit(solution)/shard_map/while/body/eval_jaxpr/ppermute | solution.py:18
  256.0 16.8 %collective-permute-start = (f32[8,128,128]{2,1,0:T(8,128)S(1)}, f32[8,128,128]{2,1,0:T(8,128)S(1)}, u32[]{:S(2)}, u32[]{:S(2)}) collective-permute-start(f32[8,128,128]{2,1,0:T(8,128)S(1)} %convolution_add_fusion.10), channel_id=1, source_target_pairs={{0,2},{2,4},{4,6},{6,8},{8,10},{10,12},{12,14},{14,16},{16,18},{18... | collective-permute-start | bytes 1572872 | tf_op jit(solution)/shard_map/while/body/eval_jaxpr/ppermute | solution.py:18
  273.6 15.9 %collective-permute-start = (f32[8,128,128]{2,1,0:T(8,128)S(1)}, f32[8,128,128]{2,1,0:T(8,128)S(1)}, u32[]{:S(2)}, u32[]{:S(2)}) collective-permute-start(f32[8,128,128]{2,1,0:T(8,128)S(1)} %convolution_add_fusion.10), channel_id=1, source_target_pairs={{0,2},{2,4},{4,6},{6,8},{8,10},{10,12},{12,14},{14,16},{16,18},{18... | collective-permute-start | bytes 1572872 | tf_op jit(solution)/shard_map/while/body/eval_jaxpr/ppermute | solution.py:18
  289.7 30.1 %copy-start.1 = (bf16[256,1024]{0,1:T(8,128)(2,1)S(1)}, bf16[256,1024]{0,1:T(8,128)(2,1)}, u32[]{:S(2)}) copy-start(bf16[256,1024]{0,1:T(8,128)(2,1)} %copy.55) | copy-start | bytes 1572868
  319.9 95.7 %collective-permute-start.3 = (bf16[2,256,1024]{1,2,0:T(8,128)(2,1)S(1)}, bf16[2,256,1024]{1,2,0:T(8,128)(2,1)}, u32[]{:S(2)}, u32[]{:S(2)}) collective-permute-start(bf16[2,256,1024]{1,2,0:T(8,128)(2,1)S(1)} %pad_maximum_fusion), channel_id=1, source_target_pairs={{0,12},{2,14},{4,16},{6,18},{8,20},{10,22},{12,24},{14,26},{16,28}... | collective-permute-start | bytes 3145736 | tf_op jit(solution)/shard_map/ppermute | solution.py:18
  321.2 96.3 %collective-permute-start.2 = (bf16[2,256,1024]{1,2,0:T(8,128)(2,1)S(1)}, bf16[2,256,1024]{1,2,0:T(8,128)(2,1)}, u32[]{:S(2)}, u32[]{:S(2)}) collective-permute-start(bf16[2,256,1024]{1,2,0:T(8,128)(2,1)S(1)} %pad_maximum_fusion), channel_id=1, source_target_pairs={{0,14},{2,16},{4,18},{6,20},{8,22},{10,24},{12,26},{14,28},{16,30}... | collective-permute-start | bytes 3145736 | tf_op jit(solution)/shard_map/ppermute | solution.py:18
  322.5 96.3 %collective-permute-start.1 = (bf16[2,256,1024]{1,2,0:T(8,128)(2,1)S(1)}, bf16[2,256,1024]{1,2,0:T(8,128)(2,1)}, u32[]{:S(2)}, u32[]{:S(2)}) collective-permute-start(bf16[2,256,1024]{1,2,0:T(8,128)(2,1)S(1)} %pad_maximum_fusion), channel_id=1, source_target_pairs={{0,16},{2,18},{4,20},{6,22},{8,24},{10,26},{12,28},{14,30},{1,17},... | collective-permute-start | bytes 3145736 | tf_op jit(solution)/shard_map/ppermute | solution.py:18
  323.8 309.1 %collective-permute-start.8 = (bf16[2,256,1024]{1,2,0:T(8,128)(2,1)S(1)}, bf16[2,256,1024]{1,2,0:T(8,128)(2,1)}, u32[]{:S(2)}, u32[]{:S(2)}) collective-permute-start(bf16[2,256,1024]{1,2,0:T(8,128)(2,1)S(1)} %pad_maximum_fusion), channel_id=1, source_target_pairs={{0,2},{2,4},{4,6},{6,8},{8,10},{10,12},{12,14},{14,16},{16,18},{18... | collective-permute-start | bytes 3145736 | tf_op jit(solution)/shard_map/ppermute | solution.py:18
  325.7 304.9 %collective-permute-start.7 = (bf16[2,256,1024]{1,2,0:T(8,128)(2,1)S(1)}, bf16[2,256,1024]{1,2,0:T(8,128)(2,1)}, u32[]{:S(2)}, u32[]{:S(2)}) collective-permute-start(bf16[2,256,1024]{1,2,0:T(8,128)(2,1)S(1)} %pad_maximum_fusion), channel_id=1, source_target_pairs={{0,4},{2,6},{4,8},{6,10},{8,12},{10,14},{12,16},{14,18},{16,20},{1... | collective-permute-start | bytes 3145736 | tf_op jit(solution)/shard_map/ppermute | solution.py:18
  415.6 212.7 %collective-permute-start.6 = (bf16[2,256,1024]{1,2,0:T(8,128)(2,1)S(1)}, bf16[2,256,1024]{1,2,0:T(8,128)(2,1)}, u32[]{:S(2)}, u32[]{:S(2)}) collective-permute-start(bf16[2,256,1024]{1,2,0:T(8,128)(2,1)S(1)} %pad_maximum_fusion), channel_id=1, source_target_pairs={{0,6},{2,8},{4,10},{6,12},{8,14},{10,16},{12,18},{14,20},{16,22},{... | collective-permute-start | bytes 3145736 | tf_op jit(solution)/shard_map/ppermute | solution.py:18
  417.5 208.5 %collective-permute-start.5 = (bf16[2,256,1024]{1,2,0:T(8,128)(2,1)S(1)}, bf16[2,256,1024]{1,2,0:T(8,128)(2,1)}, u32[]{:S(2)}, u32[]{:S(2)}) collective-permute-start(bf16[2,256,1024]{1,2,0:T(8,128)(2,1)S(1)} %pad_maximum_fusion), channel_id=1, source_target_pairs={{0,8},{2,10},{4,12},{6,14},{8,16},{10,18},{12,20},{14,22},{16,24},... | collective-permute-start | bytes 3145736 | tf_op jit(solution)/shard_map/ppermute | solution.py:18
  418.8 204.8 %collective-permute-start.4 = (bf16[2,256,1024]{1,2,0:T(8,128)(2,1)S(1)}, bf16[2,256,1024]{1,2,0:T(8,128)(2,1)}, u32[]{:S(2)}, u32[]{:S(2)}) collective-permute-start(bf16[2,256,1024]{1,2,0:T(8,128)(2,1)S(1)} %pad_maximum_fusion), channel_id=1, source_target_pairs={{0,10},{2,12},{4,14},{6,16},{8,18},{10,20},{12,22},{14,24},{16,26}... | collective-permute-start | bytes 3145736 | tf_op jit(solution)/shard_map/ppermute | solution.py:18
  661.1 12.2 %copy-start.3 = (f32[1024]{0:T(1024)S(1)}, f32[1024]{0:T(1024)}, u32[]{:S(2)}) copy-start(f32[1024]{0:T(1024)} %param.19) | copy-start | bytes 12292
where the time goes:
time: 685 us; the launch traced here: 675 us
  waiting for transfers between devices  467 us (68%)
  matrix products  106 us (15%)
  local copies, waits for them, and re-layouts  45.2 us (7%)
  starting transfers between devices  42.2 us (6%)
  other arithmetic  8.69 us (1%)
    ppermute x23, waiting for transfers between devices, shifted(): return lax.ppermute(value, axis, pairs)  467 us
    ppermute x23, starting transfers between devices, shifted(): return lax.ppermute(value, axis, pairs)  42.2 us
    unnamed x24, local copies, waits for them, and re-layouts  29 us
    sub x1, matrix products, attend_block(): exps = jnp.exp(jnp.where(allowed[None], scores - row_top, -1e+30))  16.5 us
  transfers between devices with their start and end apart: 23, of which 17 were waited for; matrix products, arithmetic and copies ran while one was open for 3% of the time, Pallas kernels for 0%

commit v1 on v0

v1 whole, which is shorter than its diff:
```python
import functools
import math

import jax
import jax.numpy as jnp
from jax import lax
from jax.experimental import pallas as pl
from jax.experimental.pallas import tpu as pltpu
from jax.sharding import PartitionSpec as P

WINDOW = 2048
HEAD = 128
PLANE = 4
F32 = jnp.float32
BF16 = jnp.bfloat16
NN = (((1,), (0,)), ((), ()))
NT = (((1,), (1,)), ((), ()))


def dot1(left, right, dims=NN):
    return lax.dot_general(left, right, dims, preferred_element_type=F32)


def split(value):
    high = value.astype(BF16)
    return high, (value - high.astype(F32)).astype(BF16)


def dot3(left, right, dims=NN):
    return (
        dot1(left[0], right[0], dims)
        + (dot1(left[0], right[1], dims) + dot1(left[1], right[0], dims))
    )


def unit_rows(entries):
    entries = entries.astype(F32)
    return entries * lax.rsqrt(jnp.sum(entries * entries, axis=-1, keepdims=True) + 1e-06)


def columns_of(head, width=HEAD):
    return pl.ds(pl.multiple_of(head * HEAD, HEAD), width)


def kernel(
    n, nh, heads, per, group, tok,
    q_ref, k_ref, v_ref, rate_ref, qa_ref, ka_ref, gain_ref,
    delta_ref, norm_ref,
    kbuf, vbuf, wbuf, scores, m_buf, c_buf, l_buf, b_buf, s_in, s_out, att, sq_out, sq_in,
    k_send, k_recv, v_send, v_recv, s_send, s_recv, sq_send, sq_recv,
):
    pos = lax.axis_index("seq")
    core = lax.axis_index("head")
    place = lax.rem(pos, PLANE)
    reach = 2 * PLANE
    chunks = heads // per
    has_up = pos + PLANE < n
    has_down = pos >= PLANE
    has_far = pos >= reach

    barrier = pltpu.get_barrier_semaphore()

    def greet(seq_index):
        pl.semaphore_signal(
            barrier, inc=1, device_id={"seq": seq_index}, device_id_type=pl.DeviceIdType.MESH
        )

    for step in range(1, PLANE):
        greet(pos - place + lax.rem(place + step, PLANE))
    for step in range(1, nh):
        pl.semaphore_signal(
            barrier, inc=1, device_id={"head": lax.rem(core + step, nh)},
            device_id_type=pl.DeviceIdType.MESH,
        )
    steps_out = jnp.logical_and(place == PLANE - 1, pos + 1 < n)
    steps_in = jnp.logical_and(place == 0, pos > 0)
    pl.when(has_up)(lambda: greet(pos + PLANE))
    pl.when(has_down)(lambda: greet(pos - PLANE))
    pl.when(steps_out)(lambda: greet(pos + 1))
    pl.when(steps_in)(lambda: greet(pos - 1))
    expected = PLANE - 1 + nh - 1
    for there in (has_up, has_down, steps_out, steps_in):
        expected = expected + there.astype(jnp.int32)
    pl.semaphore_wait(barrier, expected)

    def remote(src, dst, send_sem, recv_sem, to):
        return pltpu.make_async_remote_copy(
            src_ref=src, dst_ref=dst, send_sem=send_sem, recv_sem=recv_sem,
            device_id={"seq": to}, device_id_type=pl.DeviceIdType.MESH,
        )

    def spread(own, buf, send, recv, chunk, stage, act):
        cols = pl.ds(chunk * per * HEAD, per * HEAD)

        def one(src, index, to, reaches, cond):
            copy = remote(
                src, buf.at[reaches - 1, :, cols], send.at[index, chunk],
                recv.at[reaches - 1, chunk], to,
            )
            pl.when(cond)(lambda: act(copy))

        if stage == 0:
            src = own.at[:, cols]
            one(src, 0, pos + PLANE, PLANE, has_up)
            for step in range(1, PLANE):
                one(src, step, pos + step, step, place + step < PLANE)
        elif stage == 1:
            src = buf.at[PLANE - 1, :, cols]
            one(src, 4, pos + PLANE, reach, jnp.logical_and(has_down, has_up))
            for step in range(1, PLANE):
                one(src, 4 + step, pos + step, PLANE + step,
                    jnp.logical_and(has_down, place + step < PLANE))
                one(src, 4 + step, pos + step - PLANE, step,
                    jnp.logical_and(has_down, place + step >= PLANE))
        else:
            src = buf.at[reach - 1, :, cols]
            for step in range(1, PLANE):
                one(src, 7 + step, pos - step, reach - step,
                    jnp.logical_and(has_far, place >= step))

    def arrived(buf, recv, slot, chunk, cond):
        cols = pl.ds(chunk * per * HEAD, per * HEAD)
        here = buf.at[slot, :, cols]
        copy = pltpu.make_async_copy(here, here, recv.at[slot, chunk])
        pl.when(cond)(lambda: copy.wait())

    start = lambda copy: copy.start()
    finish = lambda copy: copy.wait_send()

    for chunk in range(chunks):
        spread(ka_ref, kbuf, k_send, k_recv, chunk, 0, start)

    for slot in range(reach):
        def clear(slot=slot):
            kbuf[slot] = jnp.zeros(kbuf.shape[1:], BF16)
            vbuf[slot] = jnp.zeros(vbuf.shape[1:], BF16)
        pl.when(pos < slot + 1)(clear)

    def clear_state():
        s_in[...] = jnp.zeros(s_in.shape, F32)
    pl.when(pos == 0)(clear_state)

    rows = lax.broadcasted_iota(jnp.int32, (tok, tok), 0)
    cols = lax.broadcasted_iota(jnp.int32, (tok, tok), 1)
    levels = tok.bit_length() - 1

    def prep(index, carry):
        apart = jnp.bitwise_xor(rows, cols)
        diagonal = (rows == cols).astype(F32)
        lane = lax.broadcasted_iota(jnp.int32, rate_ref.shape, 1)
        members = range(group)
        head_of = [index * group + i for i in members]
        q_unit = [unit_rows(q_ref[:, columns_of(h)]) for h in head_of]
        k_unit = [unit_rows(k_ref[:, columns_of(h)]) for h in head_of]
        rate = [
            jnp.sum(jnp.where(lane == h, rate_ref[...], 0.0), axis=1, keepdims=True) for h in head_of
        ]
        k_split = [split(k) for k in k_unit]
        below = [
            jnp.where(rows > cols, rate[i] * dot3(k_split[i], k_split[i], NT), 0.0) for i in members
        ]
        inverse = [diagonal - jnp.where(apart == 1, below[i], 0.0) for i in members]
        for level in range(1, levels):
            now = (apart >> level) == 1
            part = [jnp.where(now, below[i], 0.0).astype(BF16) for i in members]
            short = [inverse[i].astype(BF16) for i in members]
            inner = [dot1(part[i], short[i]).astype(BF16) for i in members]
            inverse = [inverse[i] - dot1(short[i], inner[i]) for i in members]
        rest = [
            (inverse[i] - diagonal) + dot3(split(below[i]), split(inverse[i])) for i in members
        ]
        inverse = [
            inverse[i] - dot1(inverse[i].astype(BF16), rest[i].astype(BF16)) for i in members
        ]
        targets = [
            jnp.concatenate(
                [rate[i] * k_unit[i], rate[i] * v_ref[:, columns_of(head_of[i])].astype(F32)], axis=1
            )
            for i in members
        ]
        solved = [split(dot3(split(inverse[i]), split(targets[i]))) for i in members]
        for i in members:
            h = head_of[i]
            cross = jnp.where(rows >= cols, dot3(split(q_unit[i]), k_split[i], NT), 0.0)
            mixed = dot3(split(cross), solved[i])
            l_buf[h] = q_unit[i] - mixed[:, :HEAD]
            b_buf[h] = mixed[:, HEAD:]
            moved = dot3(split(k_unit[i].T), solved[i])
            m_buf[h] = diagonal[:HEAD, :HEAD] - moved[:, :HEAD]
            c_buf[h] = moved[:, HEAD:]
        return carry

    lax.fori_loop(0, heads // group, prep, 0)

    for chunk in range(chunks):
        arrived(kbuf, k_recv, PLANE - 1, chunk, has_down)
        spread(ka_ref, kbuf, k_send, k_recv, chunk, 1, start)
    for chunk in range(chunks):
        arrived(kbuf, k_recv, reach - 1, chunk, has_far)
        spread(ka_ref, kbuf, k_send, k_recv, chunk, 2, start)

    def weigh(h, carry):
        scale = 1.0 / math.sqrt(HEAD)
        query = qa_ref[:, columns_of(h)]
        top = None
        for slot in range(reach + 1):
            keys = ka_ref[:, columns_of(h)] if slot == 0 else kbuf[slot - 1, :, columns_of(h)]
            now = dot1(query, keys, NT) * scale
            if slot == 0:
                now = jnp.where(cols <= rows, now, -1e30)
            elif slot == reach:
                now = jnp.where(jnp.logical_and(cols > rows, has_far), now, -1e30)
            else:
                now = jnp.where(pos >= slot, now, -1e30)
            scores[slot] = now
            top = now if top is None else jnp.maximum(top, now)
        top = jnp.max(top, axis=1, keepdims=True)
        total = jnp.zeros((tok, tok), F32)
        for slot in range(reach + 1):
            now = jnp.exp(scores[slot] - top)
            scores[slot] = now
            total = total + now
        scale_rows = 1.0 / jnp.sum(total, axis=1, keepdims=True)
        for slot in range(reach + 1):
            wbuf[h, slot] = (scores[slot] * scale_rows).astype(BF16)
        return carry

    late = pos >= reach + PLANE
    early_heads = jnp.where(late, heads, 0)

    def all_keys():
        for chunk in range(chunks):
            for slot in range(reach):
                if slot != PLANE - 1 and slot != reach - 1:
                    arrived(kbuf, k_recv, slot, chunk, pos >= slot + 1)

    pl.when(late)(all_keys)
    lax.fori_loop(0, early_heads, weigh, 0)

    for h in range(heads):
        state_copy = remote(s_out.at[h], s_in.at[h], s_send.at[h], s_recv.at[h], pos + 1)
        pl.when(pos > 0)(lambda: state_copy.wait_recv())
        state = split(s_in[h])

        def pass_on(h=h, state=state, state_copy=state_copy):
            s_out[h] = dot3(split(m_buf[h]), state) + c_buf[h]
            state_copy.start()
        pl.when(pos + 1 < n)(pass_on)
        delta_ref[:, columns_of(h)] = (dot3(split(l_buf[h]), state) + b_buf[h]).astype(BF16)
        if h % per == per - 1:
            spread(delta_ref, vbuf, v_send, v_recv, h // per, 0, start)

    pl.when(jnp.logical_not(late))(all_keys)
    for chunk in range(chunks):
        arrived(vbuf, v_recv, PLANE - 1, chunk, has_down)
        spread(delta_ref, vbuf, v_send, v_recv, chunk, 1, start)
    lax.fori_loop(early_heads, heads, weigh, 0)
    for chunk in range(chunks):
        arrived(vbuf, v_recv, reach - 1, chunk, has_far)
        spread(delta_ref, vbuf, v_send, v_recv, chunk, 2, start)

    squares = jnp.zeros((tok, HEAD), F32)
    for h in range(heads):
        if h % per == 0:
            for slot in range(reach):
                if slot != PLANE - 1 and slot != reach - 1:
                    arrived(vbuf, v_recv, slot, h // per, pos >= slot + 1)
        mixed = dot1(wbuf[h, 0], delta_ref[:, columns_of(h)])
        for slot in range(reach):
            mixed = mixed + dot1(wbuf[h, slot + 1], vbuf[slot, :, columns_of(h)])
        att[:, columns_of(h)] = mixed
        squares = squares + mixed * mixed
    sq_out[...] = jnp.broadcast_to(jnp.sum(squares, axis=1, keepdims=True), (tok, HEAD))
    total_sq = sq_out[...]
    trades = []
    for step in range(1, nh):
        trade = pltpu.make_async_remote_copy(
            src_ref=sq_out, dst_ref=sq_in.at[step - 1], send_sem=sq_send.at[step - 1],
            recv_sem=sq_recv.at[step - 1], device_id={"head": lax.rem(core + step, nh)},
            device_id_type=pl.DeviceIdType.MESH,
        )
        trade.start()
        trades.append(trade)
    for step, trade in enumerate(trades):
        trade.wait_recv()
        total_sq = total_sq + sq_in[step]
    scale_rows = lax.rsqrt(total_sq / (heads * HEAD * nh) + 1e-06)
    for h in range(heads):
        at = columns_of(h)
        norm_ref[:, at] = (att[:, at] * gain_ref[:, at] * scale_rows).astype(BF16)

    for trade in trades:
        trade.wait_send()
    for h in range(heads):
        state_copy = remote(s_out.at[h], s_in.at[h], s_send.at[h], s_recv.at[h], pos + 1)
        pl.when(pos + 1 < n)(lambda: state_copy.wait_send())
    for chunk in range(chunks):
        for stage in range(3):
            spread(ka_ref, kbuf, k_send, k_recv, chunk, stage, finish)
            spread(delta_ref, vbuf, v_send, v_recv, chunk, stage, finish)


def on_device(n, nh, q_delta, k_delta, v_delta, write_rate, q_attn, k_attn, out_gain):
    tok, features = q_delta.shape
    heads = write_rate.shape[1]
    per = 2 if heads % 2 == 0 else 1
    group = 4 if heads % 4 == 0 else per
    chunks = heads // per
    reach = WINDOW // tok
    assert reach == 2 * PLANE and n % PLANE == 0 and features == heads * HEAD
    vmem = pl.BlockSpec(memory_space=pltpu.VMEM)
    dma = pltpu.SemaphoreType.DMA
    return pl.pallas_call(
        functools.partial(kernel, n, nh, heads, per, group, tok),
        out_shape=[jax.ShapeDtypeStruct((tok, features), BF16)] * 2,
        in_specs=[vmem] * 7,
        out_specs=[vmem] * 2,
        scratch_shapes=[
            pltpu.VMEM((reach, tok, features), BF16),
            pltpu.VMEM((reach, tok, features), BF16),
            pltpu.VMEM((heads, reach + 1, tok, tok), BF16),
            pltpu.VMEM((reach + 1, tok, tok), F32),
            pltpu.VMEM((heads, HEAD, HEAD), F32),
            pltpu.VMEM((heads, HEAD, HEAD), F32),
            pltpu.VMEM((heads, tok, HEAD), F32),
            pltpu.VMEM((heads, tok, HEAD), F32),
            pltpu.VMEM((heads, HEAD, HEAD), F32),
            pltpu.VMEM((heads, HEAD, HEAD), F32),
            pltpu.VMEM((tok, features), F32),
            pltpu.VMEM((tok, HEAD), F32),
            pltpu.VMEM((max(nh - 1, 1), tok, HEAD), F32),
            dma((11, chunks)), dma((reach, chunks)), dma((11, chunks)), dma((reach, chunks)),
            dma((heads,)), dma((heads,)), dma((max(nh - 1, 1),)), dma((max(nh - 1, 1),)),
        ],
        compiler_params=pltpu.CompilerParams(
            collective_id=0, has_side_effects=True, vmem_limit_bytes=56 * 1024 * 1024
        ),
        cost_estimate=pl.CostEstimate(
            flops=10_000_000_000, bytes_accessed=8_000_000, transcendentals=5_000_000
        ),
    )(q_delta, k_delta, v_delta, write_rate, q_attn, k_attn, out_gain.reshape(1, features))


def solution(mesh):
    placed = (P("seq", "head"),) * 6 + (P("head"),)
    return jax.shard_map(
        functools.partial(on_device, mesh.shape["seq"], mesh.shape["head"]),
        mesh=mesh,
        in_specs=placed,
        out_specs=(P("seq", "head"), P("seq", "head")),
        check_vma=False,
    )
```

time: 685 us -> 169 us (0.25); the launches traced: 675 us -> 169 us
  waiting for transfers between devices: 467 us -> 0 us
  Pallas kernels: 0 us -> 164 us
  matrix products: 106 us -> 0 us
  starting transfers between devices: 42.2 us -> 0 us
  local copies, waits for them, and re-layouts: 45.2 us -> 4.21 us
  other arithmetic: 8.69 us -> 0 us
    ppermute x23 -> x0, waiting for transfers between devices: 467 us -> none  [shifted(): return lax.ppermute(value, axis, pairs)]
    pallas_call x0 -> x1, Pallas kernels: none -> 164 us  [on_device(): pl.pallas_call(functools.partial(kernel, n, nh, heads, per, group, tok),...]
    dot_general x62 -> x0, matrix products: 89.3 us -> none  [the longest x15 9.65 us: batched_dot(): return jnp.einsum('hij,hjk->hik', left, right, precision=highest)]
    ppermute x23 -> x0, starting transfers between devices: 42.2 us -> none  [shifted(): return lax.ppermute(value, axis, pairs)]
    unnamed x24 -> x5, local copies, waits for them, and re-layouts: 29 us -> 4.21 us
    sub x1 -> x0, matrix products: 16.5 us -> none  [attend_block(): exps = jnp.exp(jnp.where(allowed[None], scores - row_top, -1e+30))]
    slice x1 -> x0, local copies, waits for them, and re-layouts: 8.11 us -> none  [attend_block(): near_keys = rows_all[0].reshape(WINDOW + block_rows, heads_here, head_size)]
  transfers between devices with their start and end apart: 23 -> 0, of which waited for: 17 -> 0; matrix products, arithmetic and copies ran while one was open for 3% -> 0% of each run, Pallas kernels for 0% -> 0%
where the time goes in v1:
time: 169 us
  Pallas kernels  164 us (97%)
  local copies, waits for them, and re-layouts  4.21 us (2%)
    pallas_call x1, Pallas kernels, on_device(): pl.pallas_call(functools.partial(kernel, n, nh, heads, per, group, tok),...  164 us
    unnamed x5, local copies, waits for them, and re-layouts  4.21 us

profile of v1, /device:TPU:25, one launch (start us, length us, event | category | flops | bytes accessed | tf_op | source)
XLA Modules:
  0.0 168.9 jit_solution(14941292805795095569)
XLA Ops:
  0.6 1.5 copy.9.rate_ref
  2.1 164.0 %shard_map.86 = (bf16[256,1024]{1,0:T(8,128)(2,1)}, bf16[256,1024]{1,0:T(8,128)(2,1)}) custom-call(bf16[256,1024]{1,0:T(8,128)(2,1)} %q_ref.1, bf16[256,1024]{1,0:T(8,128)(2,1)} %k_ref.1, bf16[256,1024]{1,0:T(8,128)(2,1)} %v_ref.1, f32[256,8]{1,0:T(8,128)} %copy.9.rate_ref, bf16[256,1024]{1,0:T(8,128)(2,1)} %qa_ref.1, bf16[256,1024]{1,0:T(8,128)(2,1)} %ka_ref.1, ...), custom_call_target="tpu_custom_call" | custom-call | flops 10000000000 | bytes 8000000 | tf_op jit(solution)/shard_map/pallas_call | solution.py:313
  166.2 0.0 copy-start
  166.2 1.9 %copy.12 = bf16[256,1024]{1,0:T(8,128)(2,1)} copy(bf16[256,1024]{1,0:T(8,128)(2,1)} %get-tuple-element.4) | data formatting | bytes 1048576
  168.1 0.0 copy-done
  168.1 0.8 copy.13
Async XLA Ops:
  166.2 1.9 %copy-start = (bf16[256,1024]{1,0:T(8,128)(2,1)S(1)}, bf16[256,1024]{1,0:T(8,128)(2,1)}, u32[]{:S(2)}) copy-start(bf16[256,1024]{1,0:T(8,128)(2,1)} %get-tuple-element.5) | copy-start | bytes 1572868

commit v2 on v1

v2 whole, which is shorter than its diff:
```python
import functools
import math

import jax
import jax.numpy as jnp
from jax import lax
from jax.experimental import pallas as pl
from jax.experimental.pallas import tpu as pltpu
from jax.sharding import PartitionSpec as P

WINDOW = 2048
HEAD = 128
PLANE = 4
F32 = jnp.float32
BF16 = jnp.bfloat16
NN = (((1,), (0,)), ((), ()))
NT = (((1,), (1,)), ((), ()))


def dot1(left, right, dims=NN):
    return lax.dot_general(left, right, dims, preferred_element_type=F32)


def split(value):
    high = value.astype(BF16)
    return high, (value - high.astype(F32)).astype(BF16)


def dot3(left, right, dims=NN):
    return (
        dot1(left[0], right[0], dims)
        + (dot1(left[0], right[1], dims) + dot1(left[1], right[0], dims))
    )


def unit_rows(entries):
    entries = entries.astype(F32)
    return entries * lax.rsqrt(jnp.sum(entries * entries, axis=-1, keepdims=True) + 1e-06)


def columns_of(head, width=HEAD):
    return pl.ds(pl.multiple_of(head * HEAD, HEAD), width)


def kernel(
    n, nh, heads, size, reach, unroll, tok,
    q_ref, k_ref, v_ref, rate_ref, qa_ref, ka_ref, gain_ref,
    delta_ref, norm_ref,
    parts, rates, kbuf, vbuf, wbuf, scores, m_buf, c_buf, l_buf, b_buf, s_in, s_out,
    att, att_in, sq_out, sq_in,
    in_send, in_recv, k_send, k_recv, v_send, v_recv, s_send, s_recv,
    d_send, d_recv, a_send, a_recv, sq_send, sq_recv,
):
    pos = lax.axis_index("seq")
    core = lax.axis_index("head")
    place = lax.rem(pos, size)
    base = pos - place
    mine = heads // size
    wide = mine * HEAD
    back = reach // size
    units = heads
    has_up = pos + size < n
    has_down = pos >= size
    own_cols = pl.ds(pl.multiple_of(place * wide, HEAD), wide)

    barrier = pltpu.get_barrier_semaphore()

    def greet(seq_index):
        pl.semaphore_signal(
            barrier, inc=1, device_id={"seq": seq_index}, device_id_type=pl.DeviceIdType.MESH
        )

    for step in range(1, size):
        greet(base + lax.rem(place + step, size))
    for step in range(1, nh):
        pl.semaphore_signal(
            barrier, inc=1, device_id={"head": lax.rem(core + step, nh)},
            device_id_type=pl.DeviceIdType.MESH,
        )
    pl.when(has_up)(lambda: greet(pos + size))
    pl.when(has_down)(lambda: greet(pos - size))
    pl.semaphore_wait(
        barrier, size - 1 + nh - 1 + has_up.astype(jnp.int32) + has_down.astype(jnp.int32)
    )

    def remote(src, dst, send_sem, recv_sem, to):
        return pltpu.make_async_remote_copy(
            src_ref=src, dst_ref=dst, send_sem=send_sem, recv_sem=recv_sem,
            device_id={"seq": to}, device_id_type=pl.DeviceIdType.MESH,
        )

    def peer(step):
        return lax.rem(place + step, size)

    def deal(which, step):
        to = peer(step)
        if which == 5:
            src, dst = rate_ref, rates.at[place]
        else:
            ref = (k_ref, q_ref, v_ref, ka_ref, qa_ref)[which]
            src = ref.at[:, pl.ds(pl.multiple_of(to * wide, HEAD), wide)]
            dst = kbuf.at[reach + place] if which == 3 else parts.at[which, place]
        return remote(src, dst, in_send.at[which, step], in_recv.at[which, step], base + to)

    for which in (5, 0, 1, 2, 3, 4):
        for step in range(1, size):
            deal(which, step).start()
    rates[place] = rate_ref[...]
    for which, ref in enumerate((k_ref, q_ref, v_ref, ka_ref, qa_ref)):
        if which == 3:
            kbuf[reach + place] = ref[:, own_cols]
        else:
            parts[which, place] = ref[:, own_cols]

    def up(buf, send, recv, r, j):
        at = (back - r) * size + j
        return remote(
            buf.at[at], buf.at[at - size], send.at[r, j], recv.at[r, j], pos + size
        )

    def send_up(buf, send, recv, r, j):
        pl.when(jnp.logical_and(has_up, pos >= r * size))(
            lambda: up(buf, send, recv, r, j).start()
        )

    def arrived(buf, send, recv, r, j):
        pl.when(pos >= r * size)(lambda: up(buf, send, recv, r - 1, j).wait_recv())

    for r in range(1, back + 1):
        def clear(r=r):
            for j in range(size):
                kbuf[(back - r) * size + j] = jnp.zeros(kbuf.shape[1:], BF16)
                vbuf[(back - r) * size + j] = jnp.zeros(vbuf.shape[1:], BF16)
        pl.when(pos < r * size)(clear)

    def clear_state():
        s_in[...] = jnp.zeros(s_in.shape, F32)
    pl.when(jnp.logical_not(has_down))(clear_state)

    for which in (5, 0, 1, 2):
        for step in range(1, size):
            deal(which, step).wait_recv()

    rows = lax.broadcasted_iota(jnp.int32, (tok, tok), 0)
    cols = lax.broadcasted_iota(jnp.int32, (tok, tok), 1)
    levels = tok.bit_length() - 1

    def prep(index, carry):
        apart = jnp.bitwise_xor(rows, cols)
        diagonal = (rows == cols).astype(F32)
        lane = lax.broadcasted_iota(jnp.int32, rate_ref.shape, 1)
        members = range(unroll)
        unit_of = [index * unroll + i for i in members]
        block_of = [u // mine for u in unit_of]
        head_of = [lax.rem(u, mine) for u in unit_of]
        q_unit = [unit_rows(parts[1, block_of[i], :, columns_of(head_of[i])]) for i in members]
        k_unit = [unit_rows(parts[0, block_of[i], :, columns_of(head_of[i])]) for i in members]
        rate = [
            jnp.sum(
                jnp.where(lane == place * mine + head_of[i], rates[block_of[i]], 0.0),
                axis=1, keepdims=True,
            )
            for i in members
        ]
        k_split = [split(k) for k in k_unit]
        below = [
            jnp.where(rows > cols, rate[i] * dot3(k_split[i], k_split[i], NT), 0.0) for i in members
        ]
        inverse = [diagonal - jnp.where(apart == 1, below[i], 0.0) for i in members]
        for level in range(1, levels):
            now = (apart >> level) == 1
            part = [jnp.where(now, below[i], 0.0).astype(BF16) for i in members]
            short = [inverse[i].astype(BF16) for i in members]
            inner = [dot1(part[i], short[i]).astype(BF16) for i in members]
            inverse = [inverse[i] - dot1(short[i], inner[i]) for i in members]
        rest = [
            (inverse[i] - diagonal) + dot3(split(below[i]), split(inverse[i])) for i in members
        ]
        inverse = [
            inverse[i] - dot1(inverse[i].astype(BF16), rest[i].astype(BF16)) for i in members
        ]
        targets = [
            jnp.concatenate(
                [rate[i] * k_unit[i], rate[i] * parts[2, block_of[i], :, columns_of(head_of[i])].astype(F32)], axis=1
            )
            for i in members
        ]
        solved = [split(dot3(split(inverse[i]), split(targets[i]))) for i in members]
        for i in members:
            h = unit_of[i]
            cross = jnp.where(rows >= cols, dot3(split(q_unit[i]), k_split[i], NT), 0.0)
            mixed = dot3(split(cross), solved[i])
            l_buf[h] = q_unit[i] - mixed[:, :HEAD]
            b_buf[h] = mixed[:, HEAD:]
            moved = dot3(split(k_unit[i].T), solved[i])
            m_buf[h] = diagonal[:HEAD, :HEAD] - moved[:, :HEAD]
            c_buf[h] = moved[:, HEAD:]

        def keys_on():
            for step in range(1, size):
                deal(3, step).wait_recv()
            for j in range(size):
                send_up(kbuf, k_send, k_recv, 0, j)
        pl.when(index == 0)(keys_on)
        return carry

    lax.fori_loop(0, units // unroll, prep, 0)

    for step in range(1, size):
        deal(4, step).wait_recv()

    def weigh(h, carry):
        scale = 1.0 / math.sqrt(HEAD)
        block = h // mine
        at = columns_of(lax.rem(h, mine))
        query = parts[4, block, :, at]
        top = None
        for slot in range(reach + 1):
            keys = kbuf[reach + block - slot, :, at]
            now = dot1(query, keys, NT) * scale
            if slot == 0:
                now = jnp.where(cols <= rows, now, -1e30)
            elif slot == reach:
                now = jnp.where(jnp.logical_and(cols > rows, base + block >= slot), now, -1e30)
            else:
                now = jnp.where(base + block >= slot, now, -1e30)
            scores[slot] = now
            top = now if top is None else jnp.maximum(top, now)
        top = jnp.max(top, axis=1, keepdims=True)
        total = jnp.zeros((tok, tok), F32)
        for slot in range(reach + 1):
            now = jnp.exp(scores[slot] - top)
            scores[slot] = now
            total = total + now
        scale_rows = 1.0 / jnp.sum(total, axis=1, keepdims=True)
        for slot in range(reach + 1):
            wbuf[h, slot] = (scores[slot] * scale_rows).astype(BF16)
        return carry

    def state_copy(i):
        return remote(s_out.at[i], s_in.at[i], s_send.at[i], s_recv.at[i], pos + size)

    for i in range(mine):
        pl.when(has_down)(lambda: state_copy(i).wait_recv())
        state = s_in[i]
        states = []
        for j in range(size):
            states.append(split(state))
            state = dot3(split(m_buf[j * mine + i]), states[-1]) + c_buf[j * mine + i]
        s_out[i] = state
        pl.when(has_up)(lambda: state_copy(i).start())
        for j in range(size):
            u = j * mine + i
            vbuf[reach + j, :, i * HEAD:(i + 1) * HEAD] = (
                dot3(split(l_buf[u]), states[j]) + b_buf[u]
            ).astype(BF16)
    for j in range(size):
        send_up(vbuf, v_send, v_recv, 0, j)

    def give_delta(step):
        to = peer(step)
        return remote(
            vbuf.at[reach + to], delta_ref.at[:, own_cols], d_send.at[step], d_recv.at[step],
            base + to,
        )

    for step in range(1, size):
        give_delta(step).start()
    delta_ref[:, own_cols] = vbuf[reach + place]

    for r in range(1, back + 1):
        for j in range(size):
            arrived(kbuf, k_send, k_recv, r, j)
            if r < back:
                send_up(kbuf, k_send, k_recv, r, j)
    half = units // 2
    lax.fori_loop(0, half, weigh, 0)
    for r in range(1, back):
        for j in range(size):
            arrived(vbuf, v_send, v_recv, r, j)
            send_up(vbuf, v_send, v_recv, r, j)
    lax.fori_loop(half, units, weigh, 0)
    for j in range(size):
        arrived(vbuf, v_send, v_recv, back, j)

    def give_att(step):
        to = peer(step)
        return remote(
            att.at[to], att_in.at[place], a_send.at[step], a_recv.at[step], base + to
        )

    def mix(step, carry):
        block = lax.rem(place + step, size)
        for i in range(mine):
            at = slice(i * HEAD, (i + 1) * HEAD)
            mixed = jnp.zeros((tok, HEAD), F32)
            for slot in range(reach + 1):
                mixed = mixed + dot1(
                    wbuf[block * mine + i, slot], vbuf[reach + block - slot, :, at]
                )
            att[block, :, at] = mixed.astype(BF16)
        return carry

    for step in range(1, size):
        mix(step, 0)
        give_att(step).start()
    mix(0, 0)
    att_in[place] = att[place]
    for step in range(1, size):
        give_att(step).wait_recv()

    squares = jnp.zeros((tok, wide), F32)
    for j in range(size):
        now = att_in[j].astype(F32)
        squares = squares + now * now
    sq_out[...] = jnp.broadcast_to(jnp.sum(squares, axis=1, keepdims=True), (tok, HEAD))
    total_sq = sq_out[...]
    trades = []
    for step in range(1, nh):
        trade = pltpu.make_async_remote_copy(
            src_ref=sq_out, dst_ref=sq_in.at[step - 1], send_sem=sq_send.at[step - 1],
            recv_sem=sq_recv.at[step - 1], device_id={"head": lax.rem(core + step, nh)},
            device_id_type=pl.DeviceIdType.MESH,
        )
        trade.start()
        trades.append(trade)
    for step, trade in enumerate(trades):
        trade.wait_recv()
        total_sq = total_sq + sq_in[step]
    scale_rows = lax.rsqrt(total_sq / (heads * HEAD * nh) + 1e-06)
    for j in range(size):
        for i in range(mine):
            at = slice((j * mine + i) * HEAD, (j * mine + i + 1) * HEAD)
            now = att_in[j, :, i * HEAD:(i + 1) * HEAD].astype(F32)
            norm_ref[:, at] = (now * gain_ref[:, at] * scale_rows).astype(BF16)

    for trade in trades:
        trade.wait_send()
    for step in range(1, size):
        give_delta(step).wait()
        give_att(step).wait_send()
        for which in range(6):
            deal(which, step).wait_send()

    def sent_up():
        for i in range(mine):
            state_copy(i).wait_send()
        for r in range(back):
            for j in range(size):
                pl.when(pos >= r * size)(lambda: up(kbuf, k_send, k_recv, r, j).wait_send())
                pl.when(pos >= r * size)(lambda: up(vbuf, v_send, v_recv, r, j).wait_send())
    pl.when(has_up)(sent_up)


def on_device(n, nh, q_delta, k_delta, v_delta, write_rate, q_attn, k_attn, out_gain):
    tok, features = q_delta.shape
    heads = write_rate.shape[1]
    size = PLANE
    while heads % size or n % size:
        size //= 2
    mine = heads // size
    wide = mine * HEAD
    unroll = 4 if heads % 4 == 0 else 1
    reach = WINDOW // tok
    back = reach // size
    assert reach % size == 0 and features == heads * HEAD
    vmem = pl.BlockSpec(memory_space=pltpu.VMEM)
    dma = pltpu.SemaphoreType.DMA
    return pl.pallas_call(
        functools.partial(kernel, n, nh, heads, size, reach, unroll, tok),
        out_shape=[jax.ShapeDtypeStruct((tok, features), BF16)] * 2,
        in_specs=[vmem] * 7,
        out_specs=[vmem] * 2,
        scratch_shapes=[
            pltpu.VMEM((5, size, tok, wide), BF16),
            pltpu.VMEM((size, tok, heads), F32),
            pltpu.VMEM((reach + size, tok, wide), BF16),
            pltpu.VMEM((reach + size, tok, wide), BF16),
            pltpu.VMEM((heads, reach + 1, tok, tok), BF16),
            pltpu.VMEM((reach + 1, tok, tok), F32),
            pltpu.VMEM((heads, HEAD, HEAD), F32),
            pltpu.VMEM((heads, HEAD, HEAD), F32),
            pltpu.VMEM((heads, tok, HEAD), F32),
            pltpu.VMEM((heads, tok, HEAD), F32),
            pltpu.VMEM((mine, HEAD, HEAD), F32),
            pltpu.VMEM((mine, HEAD, HEAD), F32),
            pltpu.VMEM((size, tok, wide), BF16),
            pltpu.VMEM((size, tok, wide), BF16),
            pltpu.VMEM((tok, HEAD), F32),
            pltpu.VMEM((max(nh - 1, 1), tok, HEAD), F32),
            dma((6, size)), dma((6, size)),
            dma((back, size)), dma((back, size)), dma((back, size)), dma((back, size)),
            dma((mine,)), dma((mine,)), dma((size,)), dma((size,)), dma((size,)), dma((size,)),
            dma((max(nh - 1, 1),)), dma((max(nh - 1, 1),)),
        ],
        compiler_params=pltpu.CompilerParams(
            collective_id=0, has_side_effects=True, vmem_limit_bytes=56 * 1024 * 1024
        ),
        cost_estimate=pl.CostEstimate(
            flops=10_000_000_000, bytes_accessed=8_000_000, transcendentals=5_000_000
        ),
    )(q_delta, k_delta, v_delta, write_rate, q_attn, k_attn, out_gain.reshape(1, features))


def solution(mesh):
    placed = (P("seq", "head"),) * 6 + (P("head"),)
    return jax.shard_map(
        functools.partial(on_device, mesh.shape["seq"], mesh.shape["head"]),
        mesh=mesh,
        in_specs=placed,
        out_specs=(P("seq", "head"), P("seq", "head")),
        check_vma=False,
    )
```

time: 169 us -> 105 us (0.62)
  Pallas kernels: 164 us -> 100 us
    pallas_call x1, Pallas kernels: 164 us -> 100 us  [on_device(): pl.pallas_call(functools.partial(kernel, n, nh, heads, size, reach, unrol...]
where the time goes in v2:
time: 105 us
  Pallas kernels  100 us (95%)
  local copies, waits for them, and re-layouts  4.21 us (4%)
    pallas_call x1, Pallas kernels, on_device(): pl.pallas_call(functools.partial(kernel, n, nh, heads, size, reach, unrol...  100 us
    unnamed x5, local copies, waits for them, and re-layouts  4.21 us

profile of v2, /device:TPU:25, one launch (start us, length us, event | category | flops | bytes accessed | tf_op | source)
XLA Modules:
  0.0 105.1 jit_solution(5246224595598003118)
XLA Ops:
  0.6 1.5 %copy.9.rate_ref = f32[256,8]{1,0:T(8,128)} copy(f32[256,8]{0,1:T(8,128)} %param.10) | data formatting | bytes 16384 | tf_op args[3]
  2.1 100.2 %shard_map.86 = (bf16[256,1024]{1,0:T(8,128)(2,1)}, bf16[256,1024]{1,0:T(8,128)(2,1)}) custom-call(bf16[256,1024]{1,0:T(8,128)(2,1)} %q_ref.1, bf16[256,1024]{1,0:T(8,128)(2,1)} %k_ref.1, bf16[256,1024]{1,0:T(8,128)(2,1)} %v_ref.1, f32[256,8]{1,0:T(8,128)} %copy.9.rate_ref, bf16[256,1024]{1,0:T(8,128)(2,1)} %qa_ref.1, bf16[256,1024]{1,0:T(8,128)(2,1)} %ka_ref.1, ...), custom_call_target="tpu_custom_call" | custom-call | flops 10000000000 | bytes 8000000 | tf_op jit(solution)/shard_map/pallas_call | solution.py:369
  102.3 0.0 copy-start
  102.3 1.9 %copy.12 = bf16[256,1024]{1,0:T(8,128)(2,1)} copy(bf16[256,1024]{1,0:T(8,128)(2,1)} %get-tuple-element.4) | data formatting | bytes 1048576
  104.3 0.0 copy-done
  104.3 0.8 copy.13
Async XLA Ops:
  102.3 1.9 %copy-start = (bf16[256,1024]{1,0:T(8,128)(2,1)S(1)}, bf16[256,1024]{1,0:T(8,128)(2,1)}, u32[]{:S(2)}) copy-start(bf16[256,1024]{1,0:T(8,128)(2,1)} %get-tuple-element.5) | copy-start | bytes 1572868

commit v3 on v2

--- a/solution.py
+++ b/solution.py
@@ -46,7 +46,7 @@
     n, nh, heads, size, reach, unroll, tok,
     q_ref, k_ref, v_ref, rate_ref, qa_ref, ka_ref, gain_ref,
     delta_ref, norm_ref,
-    parts, rates, kbuf, vbuf, wbuf, scores, m_buf, c_buf, l_buf, b_buf, s_in, s_out,
+    parts, rates, kbuf, vbuf, wbuf, scores, m_buf, c_buf, l_buf, b_buf, s_in, s_out, t_buf,
     att, att_in, sq_out, sq_in,
     in_send, in_recv, k_send, k_recv, v_send, v_recv, s_send, s_recv,
     d_send, d_recv, a_send, a_recv, sq_send, sq_recv,
@@ -102,8 +102,8 @@
             dst = kbuf.at[reach + place] if which == 3 else parts.at[which, place]
         return remote(src, dst, in_send.at[which, step], in_recv.at[which, step], base + to)
 
-    for which in (5, 0, 1, 2, 3, 4):
-        for step in range(1, size):
+    for step in range(1, size):
+        for which in (5, 0, 1, 2):
             deal(which, step).start()
     rates[place] = rate_ref[...]
     for which, ref in enumerate((k_ref, q_ref, v_ref, ka_ref, qa_ref)):
@@ -137,9 +137,13 @@
         s_in[...] = jnp.zeros(s_in.shape, F32)
     pl.when(jnp.logical_not(has_down))(clear_state)
 
-    for which in (5, 0, 1, 2):
+    first = unroll // mine
+    for step in range(1, first):
+        for which in (5, 0, 1, 2):
+            deal(which, step).wait_recv()
+    for which in (3, 4):
         for step in range(1, size):
-            deal(which, step).wait_recv()
+            deal(which, step).start()
 
     rows = lax.broadcasted_iota(jnp.int32, (tok, tok), 0)
     cols = lax.broadcasted_iota(jnp.int32, (tok, tok), 1)
@@ -150,9 +154,10 @@
         diagonal = (rows == cols).astype(F32)
         lane = lax.broadcasted_iota(jnp.int32, rate_ref.shape, 1)
         members = range(unroll)
-        unit_of = [index * unroll + i for i in members]
-        block_of = [u // mine for u in unit_of]
-        head_of = [lax.rem(u, mine) for u in unit_of]
+        turn_of = [index * unroll + i for i in members]
+        head_of = [lax.rem(u, mine) for u in turn_of]
+        block_of = [lax.rem(place - u // mine + size, size) for u in turn_of]
+        unit_of = [block_of[i] * mine + head_of[i] for i in members]
         q_unit = [unit_rows(parts[1, block_of[i], :, columns_of(head_of[i])]) for i in members]
         k_unit = [unit_rows(parts[0, block_of[i], :, columns_of(head_of[i])]) for i in members]
         rate = [
@@ -197,6 +202,9 @@
             c_buf[h] = moved[:, HEAD:]
 
         def keys_on():
+            for step in range(first, size):
+                for which in (5, 0, 1, 2):
+                    deal(which, step).wait_recv()
             for step in range(1, size):
                 deal(3, step).wait_recv()
             for j in range(size):
@@ -211,6 +219,7 @@
 
     def weigh(h, carry):
         scale = 1.0 / math.sqrt(HEAD)
+        h = units - 1 - h
         block = h // mine
         at = columns_of(lax.rem(h, mine))
         query = parts[4, block, :, at]
@@ -240,20 +249,45 @@
     def state_copy(i):
         return remote(s_out.at[i], s_in.at[i], s_send.at[i], s_recv.at[i], pos + size)
 
+    whole = [jnp.concatenate([m_buf[i], c_buf[i]], axis=1) for i in range(mine)]
+    for j in range(1, size):
+        for i in range(mine):
+            u = j * mine + i
+            moved = dot3(split(m_buf[u]), split(whole[i]))
+            whole[i] = jnp.concatenate([moved[:, :HEAD], moved[:, HEAD:] + c_buf[u]], axis=1)
+    for i in range(mine):
+        t_buf[i] = whole[i]
+
+    for r in range(1, back):
+        for j in range(size):
+            arrived(kbuf, k_send, k_recv, r, j)
+            send_up(kbuf, k_send, k_recv, r, j)
+
+    last = jnp.logical_and(has_down, jnp.logical_not(has_up))
+    some = jnp.where(pos >= reach, units // 4, 0)
+    early = jnp.where(last, units, some)
+
+    def far_keys():
+        for j in range(size):
+            arrived(kbuf, k_send, k_recv, back, j)
+
+    pl.when(early > 0)(far_keys)
+    lax.fori_loop(0, early, weigh, 0)
+
     for i in range(mine):
         pl.when(has_down)(lambda: state_copy(i).wait_recv())
-        state = s_in[i]
-        states = []
-        for j in range(size):
-            states.append(split(state))
-            state = dot3(split(m_buf[j * mine + i]), states[-1]) + c_buf[j * mine + i]
-        s_out[i] = state
+        s_out[i] = dot3(split(t_buf[i, :, :HEAD]), split(s_in[i])) + t_buf[i, :, HEAD:]
         pl.when(has_up)(lambda: state_copy(i).start())
-        for j in range(size):
+    state = [s_in[i] for i in range(mine)]
+    for j in range(size):
+        for i in range(mine):
             u = j * mine + i
+            now = split(state[i])
             vbuf[reach + j, :, i * HEAD:(i + 1) * HEAD] = (
-                dot3(split(l_buf[u]), states[j]) + b_buf[u]
+                dot3(split(l_buf[u]), now) + b_buf[u]
             ).astype(BF16)
+            if j + 1 < size:
+                state[i] = dot3(split(m_buf[u]), now) + c_buf[u]
     for j in range(size):
         send_up(vbuf, v_send, v_recv, 0, j)
 
@@ -268,13 +302,9 @@
         give_delta(step).start()
     delta_ref[:, own_cols] = vbuf[reach + place]
 
-    for r in range(1, back + 1):
-        for j in range(size):
-            arrived(kbuf, k_send, k_recv, r, j)
-            if r < back:
-                send_up(kbuf, k_send, k_recv, r, j)
-    half = units // 2
-    lax.fori_loop(0, half, weigh, 0)
+    pl.when(early == 0)(far_keys)
+    half = early + (units - early) // 2
+    lax.fori_loop(early, half, weigh, 0)
     for r in range(1, back):
         for j in range(size):
             arrived(vbuf, v_send, v_recv, r, j)
@@ -384,6 +414,7 @@
             pltpu.VMEM((heads, tok, HEAD), F32),
             pltpu.VMEM((mine, HEAD, HEAD), F32),
             pltpu.VMEM((mine, HEAD, HEAD), F32),
+            pltpu.VMEM((mine, HEAD, 2 * HEAD), F32),
             pltpu.VMEM((size, tok, wide), BF16),
             pltpu.VMEM((size, tok, wide), BF16),
             pltpu.VMEM((tok, HEAD), F32),

time: 105 us -> 101 us (0.962)
  Pallas kernels: 100 us -> 95.5 us
    pallas_call x1, Pallas kernels: 100 us -> 95.5 us  [on_device(): pl.pallas_call(functools.partial(kernel, n, nh, heads, size, reach, unrol...]
where the time goes in v3:
time: 101 us; the launch traced here: 100 us
  Pallas kernels  95.5 us (95%)
  local copies, waits for them, and re-layouts  4.21 us (4%)
    pallas_call x1, Pallas kernels, on_device(): pl.pallas_call(functools.partial(kernel, n, nh, heads, size, reach, unrol...  95.5 us
    unnamed x5, local copies, waits for them, and re-layouts  4.21 us

profile of v3, /device:TPU:25, one launch (start us, length us, event | category | flops | bytes accessed | tf_op | source)
XLA Modules:
  0.0 100.4 jit_solution(3861581368066301416)
XLA Ops:
  0.6 1.5 %copy.9.rate_ref = f32[256,8]{1,0:T(8,128)} copy(f32[256,8]{0,1:T(8,128)} %param.10) | data formatting | bytes 16384 | tf_op args[3]
  2.1 95.5 %shard_map.86 = (bf16[256,1024]{1,0:T(8,128)(2,1)}, bf16[256,1024]{1,0:T(8,128)(2,1)}) custom-call(bf16[256,1024]{1,0:T(8,128)(2,1)} %q_ref.1, bf16[256,1024]{1,0:T(8,128)(2,1)} %k_ref.1, bf16[256,1024]{1,0:T(8,128)(2,1)} %v_ref.1, f32[256,8]{1,0:T(8,128)} %copy.9.rate_ref, bf16[256,1024]{1,0:T(8,128)(2,1)} %qa_ref.1, bf16[256,1024]{1,0:T(8,128)(2,1)} %ka_ref.1, ...), custom_call_target="tpu_custom_call" | custom-call | flops 10000000000 | bytes 8000000 | tf_op jit(solution)/shard_map/pallas_call | solution.py:399
  97.6 0.0 copy-start
  97.6 1.9 %copy.12 = bf16[256,1024]{1,0:T(8,128)(2,1)} copy(bf16[256,1024]{1,0:T(8,128)(2,1)} %get-tuple-element.4) | data formatting | bytes 1048576
  99.6 0.0 copy-done
  99.6 0.8 copy.13
Async XLA Ops:
  97.6 1.9 %copy-start = (bf16[256,1024]{1,0:T(8,128)(2,1)S(1)}, bf16[256,1024]{1,0:T(8,128)(2,1)}, u32[]{:S(2)}) copy-start(bf16[256,1024]{1,0:T(8,128)(2,1)} %get-tuple-element.5) | copy-start | bytes 1572868

commit v4 on v3

--- a/solution.py
+++ b/solution.py
@@ -288,7 +288,6 @@
             ).astype(BF16)
             if j + 1 < size:
                 state[i] = dot3(split(m_buf[u]), now) + c_buf[u]
-    for j in range(size):
         send_up(vbuf, v_send, v_recv, 0, j)
 
     def give_delta(step):
@@ -303,7 +302,7 @@
     delta_ref[:, own_cols] = vbuf[reach + place]
 
     pl.when(early == 0)(far_keys)
-    half = early + (units - early) // 2
+    half = early + (units - early) // 4
     lax.fori_loop(early, half, weigh, 0)
     for r in range(1, back):
         for j in range(size):

time: 101 us -> 101 us (level)
  no operation moved by 1% of the time
where the time goes in v4:
time: 101 us; the launch traced here: 100 us
  Pallas kernels  95.3 us (94%)
  local copies, waits for them, and re-layouts  4.21 us (4%)
    pallas_call x1, Pallas kernels, on_device(): pl.pallas_call(functools.partial(kernel, n, nh, heads, size, reach, unrol...  95.3 us
    unnamed x5, local copies, waits for them, and re-layouts  4.21 us

profile of v4, /device:TPU:25, one launch (start us, length us, event | category | flops | bytes accessed | tf_op | source)
XLA Modules:
  0.0 100.2 jit_solution(11113101964569103017)
XLA Ops:
  0.6 1.5 %copy.9.rate_ref = f32[256,8]{1,0:T(8,128)} copy(f32[256,8]{0,1:T(8,128)} %param.10) | data formatting | bytes 16384 | tf_op args[3]
  2.1 95.3 %shard_map.86 = (bf16[256,1024]{1,0:T(8,128)(2,1)}, bf16[256,1024]{1,0:T(8,128)(2,1)}) custom-call(bf16[256,1024]{1,0:T(8,128)(2,1)} %q_ref.1, bf16[256,1024]{1,0:T(8,128)(2,1)} %k_ref.1, bf16[256,1024]{1,0:T(8,128)(2,1)} %v_ref.1, f32[256,8]{1,0:T(8,128)} %copy.9.rate_ref, bf16[256,1024]{1,0:T(8,128)(2,1)} %qa_ref.1, bf16[256,1024]{1,0:T(8,128)(2,1)} %ka_ref.1, ...), custom_call_target="tpu_custom_call" | custom-call | flops 10000000000 | bytes 8000000 | tf_op jit(solution)/shard_map/pallas_call | solution.py:398
  97.4 0.0 copy-start
  97.4 1.9 %copy.12 = bf16[256,1024]{1,0:T(8,128)(2,1)} copy(bf16[256,1024]{1,0:T(8,128)(2,1)} %get-tuple-element.4) | data formatting | bytes 1048576
  99.4 0.0 copy-done
  99.4 0.8 copy.13
Async XLA Ops:
  97.4 1.9 %copy-start = (bf16[256,1024]{1,0:T(8,128)(2,1)S(1)}, bf16[256,1024]{1,0:T(8,128)(2,1)}, u32[]{:S(2)}) copy-start(bf16[256,1024]{1,0:T(8,128)(2,1)} %get-tuple-element.5) | copy-start | bytes 1572868
